TPU v7x, 32 devices: a whole 2x2x4 slice. The times are simulated.
32 devices in a mesh: replica: 2 (over core), shard: 16 (over z, y, x).
Axes of the slice: x: 2, y: 2, z: 4, core: 2. Of those that a mesh axis runs over, the one named last changes fastest.
Arguments:
- features: bfloat16 [64, 544, 512], P(('replica', 'shard')), may hold values from -20 to 20
- frame_times: int32 [64, 544], P(('replica', 'shard')), may hold values from 0 to 1692, as said below
- cotangent: bfloat16 [64, 544, 512], P(('replica', 'shard')), may hold values from -20 to 20
- vectors: bfloat16 [9, 512], P(None, 'shard'), may hold values from 0.25 to 1.75
- first_up: bfloat16 [512, 2048], P('shard'), may hold values from -0.25 to 0.25
- first_down: bfloat16 [2048, 512], P('shard'), may hold values from -0.25 to 0.25
- query_key_value: bfloat16 [512, 1536], P('shard'), may hold values from -0.25 to 0.25
- place_weight: bfloat16 [512, 512], P('shard'), may hold values from -0.25 to 0.25
- out_weight: bfloat16 [512, 512], P('shard'), may hold values from -1 to 1
- point_glu: bfloat16 [512, 1024], P('shard'), may hold values from -0.25 to 0.25
- depth_taps: bfloat16 [31, 512], P(None, 'shard'), may hold values from -1 to 1
- point_out: bfloat16 [512, 512], P('shard'), may hold values from -0.5 to 0.5
- second_up: bfloat16 [512, 2048], P('shard'), may hold values from -0.25 to 0.25
- second_down: bfloat16 [2048, 512], P('shard'), may hold values from -0.25 to 0.25
Outputs:
- output: bfloat16 [64, 544, 512], P(('replica', 'shard'))
- grad_features: bfloat16 [64, 544, 512], P(('replica', 'shard'))
- grad_vectors: float32 [9, 512], P(None, 'shard')
- grad_first_up: float32 [512, 2048], P('shard')
- grad_first_down: float32 [2048, 512], P('shard')
- grad_query_key_value: float32 [512, 1536], P('shard')
- grad_place_weight: float32 [512, 512], P('shard')
- grad_out_weight: float32 [512, 512], P('shard')
- grad_point_glu: float32 [512, 1024], P('shard')
- grad_depth_taps: float32 [31, 512], P(None, 'shard')
- grad_point_out: float32 [512, 512], P('shard')
- grad_second_up: float32 [512, 2048], P('shard')
- grad_second_down: float32 [2048, 512], P('shard')
Inputs may be any that keep to these rules, and one draw needn't show every extreme that they name: `frame_times`: within a clip the frame times rise by 1 to 3 from each token to the next.
All inputs are finite; a program needn't handle non-finite values.
Results may differ from a plain program's by a relative error of at most 0.04.
Values may be sent and summed in bfloat16 or wider, within the bound.
A program may use at most 256 MiB of HBM per device.

v0:
```python
import math

import jax
import jax.numpy as jnp
from jax import lax
from jax.sharding import PartitionSpec as P

HEADS = 8
HEAD_DIM = 64


epsilon = 1e-05


def normalize(values, gain_row):
    center = values - jnp.mean(values, axis=-1, keepdims=True)
    spread = jnp.mean(center * center, axis=-1, keepdims=True)
    return center * lax.rsqrt(spread + epsilon) * gain_row


def normalize_back(values, gain_row, grad_normed):
    pull = jax.vjp(normalize, values, gain_row)[1]
    return pull(grad_normed)


def swish_act(values):
    return values * jax.nn.sigmoid(values)


def swish_slope(values):
    sigmoid = jax.nn.sigmoid(values)
    return sigmoid * (1.0 + values * (1.0 - sigmoid))


def wave_table(frame_pos, model_width):
    half_width = model_width // 2
    frequency = jnp.exp(
        jnp.arange(half_width, dtype=jnp.float32) * (-math.log(10000.0) / half_width)
    )
    angles = frame_pos.astype(jnp.float32)[:, None] * frequency[None, :]
    return (jnp.sin(angles), jnp.cos(angles))


def depthwise(gated_rows, tap_weights):
    tap_count = tap_weights.shape[0]
    reach_left = tap_count // 2
    clip_length = gated_rows.shape[1]
    padded = jnp.pad(gated_rows, ((0, 0), (reach_left, tap_count - 1 - reach_left), (0, 0)))
    running_sum = jnp.zeros_like(gated_rows)
    for offset in range(tap_count):
        running_sum = running_sum + tap_weights[offset] * padded[:, offset : offset + clip_length]
    return running_sum


def gated_conv(mixed_rows, tap_weights):
    half_width = mixed_rows.shape[-1] // 2
    gated_rows = mixed_rows[..., :half_width] * jax.nn.sigmoid(mixed_rows[..., half_width:])
    return depthwise(gated_rows, tap_weights)


def product(left_side, right_side):
    return jnp.dot(left_side, right_side, preferred_element_type=jnp.float32)


def product_left(left_side, right_side):
    return lax.dot_general(
        left_side, right_side, (((0,), (0,)), ((), ())), preferred_element_type=jnp.float32
    )


def product_right(left_side, right_side):
    return lax.dot_general(
        left_side, right_side, (((1,), (1,)), ((), ())), preferred_element_type=jnp.float32
    )


def feed_forward(inputs, gain_row, up_full, down_full):
    normed_low = normalize(inputs, gain_row).astype(jnp.bfloat16)
    hidden = product(normed_low, up_full)
    active_low = swish_act(hidden).astype(jnp.bfloat16)
    return (product(active_low, down_full), (normed_low, hidden, active_low))


def feed_back(grad_stream, inputs, gain_row, up_full, down_full, kept_values):
    normed_low, hidden, active_low = kept_values
    grad_low = (0.5 * grad_stream).astype(jnp.bfloat16)
    grad_down = product_left(active_low, grad_low)
    grad_hidden = (product_right(grad_low, down_full) * swish_slope(hidden)).astype(jnp.bfloat16)
    grad_up = product_left(normed_low, grad_hidden)
    grad_normed = product_right(grad_hidden, up_full)
    grad_extra, grad_gain = normalize_back(inputs, gain_row, grad_normed)
    return (grad_stream + grad_extra, grad_gain, grad_up, grad_down)


def clip_inputs(joint_rows, u_bias, v_bias):
    clip_length = joint_rows.shape[0]
    model_width = joint_rows.shape[1] // 3
    head_shape = (clip_length, HEADS, model_width // HEADS)
    query = joint_rows[:, :model_width]
    query_u = (query + u_bias).reshape(head_shape).astype(jnp.bfloat16)
    query_v = (query + v_bias).reshape(head_shape).astype(jnp.bfloat16)
    key_low = joint_rows[:, model_width : 2 * model_width].reshape(head_shape).astype(jnp.bfloat16)
    value_low = joint_rows[:, 2 * model_width :].reshape(head_shape).astype(jnp.bfloat16)
    return (query_u, query_v, key_low, value_low)


def clip_scores(query_u, query_v, key_low, place3, frame_pos):
    sine_rows, cosines = wave_table(frame_pos, place3.shape[0])
    raw_place = jnp.einsum("ihd,ehd->hie", query_v, place3, preferred_element_type=jnp.float32)
    half_width = raw_place.shape[-1] // 2
    part_sin = raw_place[..., :half_width]
    part_cos = raw_place[..., half_width:]
    coeff_low = jnp.concatenate(
        [part_sin * sine_rows + part_cos * cosines, part_cos * sine_rows - part_sin * cosines],
        axis=-1,
    ).astype(jnp.bfloat16)
    basis_low = jnp.concatenate([cosines, sine_rows], axis=-1).astype(jnp.bfloat16)
    content = jnp.einsum("ihd,jhd->hij", query_u, key_low, preferred_element_type=jnp.float32)
    placed = jnp.einsum("hie,je->hij", coeff_low, basis_low, preferred_element_type=jnp.float32)
    scores = (content + placed) * (1.0 / math.sqrt(HEAD_DIM))
    return (scores, sine_rows, cosines, basis_low)


def clip_forward(joint_rows, frame_pos, u_bias, v_bias, place3):
    query_u, query_v, key_low, value_low = clip_inputs(joint_rows, u_bias, v_bias)
    scores = clip_scores(query_u, query_v, key_low, place3, frame_pos)[0]
    row_peak = jnp.max(scores, axis=-1, keepdims=True)
    logsum = row_peak + jnp.log(jnp.sum(jnp.exp(scores - row_peak), axis=-1, keepdims=True))
    probs_low = jnp.exp(scores - logsum).astype(jnp.bfloat16)
    context = jnp.einsum("hij,jhd->ihd", probs_low, value_low, preferred_element_type=jnp.float32)
    return (context.reshape(joint_rows.shape[0], -1).astype(jnp.bfloat16), logsum)


def clip_backward(joint_rows, frame_pos, logsum, grad_context, u_bias, v_bias, place3):
    clip_length = joint_rows.shape[0]
    query_u, query_v, key_low, value_low = clip_inputs(joint_rows, u_bias, v_bias)
    scores, sine_rows, cosines, basis_low = clip_scores(
        query_u, query_v, key_low, place3, frame_pos
    )
    prob_values = jnp.exp(scores - logsum)
    probs_low = prob_values.astype(jnp.bfloat16)
    grad_heads = grad_context.reshape(query_u.shape)
    grad_value = jnp.einsum(
        "hij,ihd->jhd", probs_low, grad_heads, preferred_element_type=jnp.float32
    )
    grad_probs = jnp.einsum(
        "ihd,jhd->hij", grad_heads, value_low, preferred_element_type=jnp.float32
    )
    inner_sum = jnp.sum(grad_probs * prob_values, axis=-1, keepdims=True)
    grad_scores = (prob_values * (grad_probs - inner_sum)).astype(jnp.bfloat16) * (
        1.0 / math.sqrt(HEAD_DIM)
    )
    grad_query_u = jnp.einsum(
        "hij,jhd->ihd", grad_scores, key_low, preferred_element_type=jnp.float32
    )
    grad_key = jnp.einsum("hij,ihd->jhd", grad_scores, query_u, preferred_element_type=jnp.float32)
    grad_coeff = jnp.einsum(
        "hij,je->hie", grad_scores, basis_low, preferred_element_type=jnp.float32
    )
    half_width = grad_coeff.shape[-1] // 2
    grad_cos_part = grad_coeff[..., :half_width]
    grad_sin_part = grad_coeff[..., half_width:]
    grad_raw = jnp.concatenate(
        [
            grad_cos_part * sine_rows - grad_sin_part * cosines,
            grad_cos_part * cosines + grad_sin_part * sine_rows,
        ],
        axis=-1,
    ).astype(jnp.bfloat16)
    grad_query_v = jnp.einsum("hie,ehd->ihd", grad_raw, place3, preferred_element_type=jnp.float32)
    grad_place = jnp.einsum("hie,ihd->ehd", grad_raw, query_v, preferred_element_type=jnp.float32)
    grad_joint = jnp.concatenate(
        [
            (grad_query_u + grad_query_v).reshape(clip_length, -1),
            grad_key.reshape(clip_length, -1),
            grad_value.reshape(clip_length, -1),
        ],
        axis=-1,
    )
    return (
        grad_joint,
        jnp.sum(grad_query_u, axis=0).reshape(-1),
        jnp.sum(grad_query_v, axis=0).reshape(-1),
        grad_place,
    )


def body(
    features,
    frame_times,
    cotangent,
    vectors,
    first_up,
    first_down,
    query_key_value,
    place_weight,
    out_weight,
    point_glu,
    depth_taps,
    point_out,
    second_up,
    second_down,
):
    clip_count, clip_length, model_width = features.shape
    row_count = clip_count * clip_length
    token_count = row_count * lax.axis_size("replica") * lax.axis_size("shard")

    def first_block():
        return (
            lax.all_gather(vectors, "shard", axis=1, tiled=True),
            lax.all_gather(first_up, "shard", axis=0, tiled=True),
            lax.all_gather(first_down, "shard", axis=0, tiled=True),
        )

    def attend_block():
        return (
            lax.all_gather(query_key_value, "shard", axis=0, tiled=True),
            lax.all_gather(place_weight, "shard", axis=0, tiled=True),
            lax.all_gather(out_weight, "shard", axis=0, tiled=True),
        )

    def conv_block():
        return (
            lax.all_gather(point_glu, "shard", axis=0, tiled=True),
            lax.all_gather(depth_taps, "shard", axis=1, tiled=True),
            lax.all_gather(point_out, "shard", axis=0, tiled=True),
        )

    def second_block():
        return (
            lax.all_gather(second_up, "shard", axis=0, tiled=True),
            lax.all_gather(second_down, "shard", axis=0, tiled=True),
        )

    first_full = first_block()
    gains = first_full[0].astype(jnp.float32)
    inputs = features.reshape(row_count, model_width).astype(jnp.float32)
    first_out, first_kept = feed_forward(inputs, gains[0], first_full[1], first_full[2])
    after_first = inputs + 0.5 * first_out
    attend_full = attend_block()
    normed_attend = normalize(after_first, gains[1]).astype(jnp.bfloat16)
    joint_rows = product(normed_attend, attend_full[0])
    joint_clips = joint_rows.reshape(clip_count, clip_length, 3 * model_width)
    place_full = attend_full[1].reshape(model_width, HEADS, model_width // HEADS)

    def forward_clip(clip_item):
        return clip_forward(clip_item[0], clip_item[1], gains[2], gains[3], place_full)

    context_clips, logsum_clips = lax.map(forward_clip, (joint_clips, frame_times))
    context_low = context_clips.reshape(row_count, model_width)
    after_attend = after_first + product(context_low, attend_full[2])
    conv_full = conv_block()
    normed_conv = normalize(after_attend, gains[4]).astype(jnp.bfloat16)
    mixed_rows = product(normed_conv, conv_full[0]).reshape(
        clip_count, clip_length, 2 * model_width
    )
    conv_flat = gated_conv(mixed_rows, conv_full[1].astype(jnp.float32)).reshape(
        row_count, model_width
    )
    channel_mean = lax.psum(jnp.sum(conv_flat, axis=0), ("replica", "shard")) / token_count
    centered = conv_flat - channel_mean
    variance = lax.psum(jnp.sum(centered * centered, axis=0), ("replica", "shard")) / token_count
    inverse = lax.rsqrt(variance + epsilon)
    unit_values = centered * inverse
    shaped = unit_values * gains[5] + gains[6]
    active_conv = swish_act(shaped).astype(jnp.bfloat16)
    after_conv = after_attend + product(active_conv, conv_full[2])
    second_full = second_block()
    second_out, second_kept = feed_forward(after_conv, gains[7], second_full[0], second_full[1])
    after_second = after_conv + 0.5 * second_out
    output = normalize(after_second, gains[8])
    grad_last, grad_final_gain = normalize_back(
        after_second, gains[8], cotangent.reshape(row_count, model_width).astype(jnp.float32)
    )
    second_back = second_block()
    grad_conv_out, grad_second_gain, grad_second_up, grad_second_down = feed_back(
        grad_last, after_conv, gains[7], second_back[0], second_back[1], second_kept
    )
    second_shards = (
        lax.psum_scatter(
            grad_second_up.astype(jnp.bfloat16), "shard", scatter_dimension=0, tiled=True
        ).astype(jnp.float32),
        lax.psum_scatter(
            grad_second_down.astype(jnp.bfloat16), "shard", scatter_dimension=0, tiled=True
        ).astype(jnp.float32),
    )
    conv_back = conv_block()
    grad_low = grad_conv_out.astype(jnp.bfloat16)
    grad_point_out = product_left(active_conv, grad_low)
    grad_shaped = product_right(grad_low, conv_back[2]) * swish_slope(shaped)
    shift_total, gain_total = lax.psum(
        (jnp.sum(grad_shaped, axis=0), jnp.sum(grad_shaped * unit_values, axis=0)),
        ("replica", "shard"),
    )
    grad_conv = (
        gains[5]
        * inverse
        * (grad_shaped - shift_total / token_count - unit_values * (gain_total / token_count))
    )
    pull_conv = jax.vjp(gated_conv, mixed_rows, conv_back[1].astype(jnp.float32))[1]
    grad_mixed, grad_taps = pull_conv(grad_conv.reshape(clip_count, clip_length, model_width))
    grad_mixed_low = grad_mixed.reshape(row_count, 2 * model_width).astype(jnp.bfloat16)
    grad_point_glu = product_left(normed_conv, grad_mixed_low)
    grad_extra, grad_conv_gain = normalize_back(
        after_attend, gains[4], product_right(grad_mixed_low, conv_back[0])
    )
    grad_attend_out = grad_conv_out + grad_extra
    conv_shards = (
        lax.psum_scatter(
            grad_point_glu.astype(jnp.bfloat16), "shard", scatter_dimension=0, tiled=True
        ).astype(jnp.float32),
        lax.psum_scatter(
            grad_taps.astype(jnp.bfloat16), "shard", scatter_dimension=1, tiled=True
        ).astype(jnp.float32),
        lax.psum_scatter(
            grad_point_out.astype(jnp.bfloat16), "shard", scatter_dimension=0, tiled=True
        ).astype(jnp.float32),
    )
    attend_back = attend_block()
    grad_low = grad_attend_out.astype(jnp.bfloat16)
    grad_out_weight = product_left(context_low, grad_low)
    grad_context = (
        product_right(grad_low, attend_back[2])
        .astype(jnp.bfloat16)
        .reshape(clip_count, clip_length, model_width)
    )
    place_back = attend_back[1].reshape(model_width, HEADS, model_width // HEADS)

    def backward_clip(running, clip_item):
        grad_joint, grad_u, grad_v, grad_place = clip_backward(
            clip_item[0], clip_item[1], clip_item[2], clip_item[3], gains[2], gains[3], place_back
        )
        return ((running[0] + grad_u, running[1] + grad_v, running[2] + grad_place), grad_joint)

    start_sums = (
        jnp.zeros((model_width,), jnp.float32),
        jnp.zeros((model_width,), jnp.float32),
        jnp.zeros(place_back.shape, jnp.float32),
    )
    bias_sums, grad_joint_clips = lax.scan(
        backward_clip, start_sums, (joint_clips, frame_times, logsum_clips, grad_context)
    )
    grad_joint_low = grad_joint_clips.reshape(row_count, 3 * model_width).astype(jnp.bfloat16)
    grad_qkv = product_left(normed_attend, grad_joint_low)
    grad_extra, grad_attend_gain = normalize_back(
        after_first, gains[1], product_right(grad_joint_low, attend_back[0])
    )
    grad_first_out = grad_attend_out + grad_extra
    grad_place_full = bias_sums[2].reshape(model_width, model_width)
    attend_shards = (
        lax.psum_scatter(
            grad_qkv.astype(jnp.bfloat16), "shard", scatter_dimension=0, tiled=True
        ).astype(jnp.float32),
        lax.psum_scatter(
            grad_place_full.astype(jnp.bfloat16), "shard", scatter_dimension=0, tiled=True
        ).astype(jnp.float32),
        lax.psum_scatter(
            grad_out_weight.astype(jnp.bfloat16), "shard", scatter_dimension=0, tiled=True
        ).astype(jnp.float32),
    )
    first_back = first_block()
    first_gains = first_back[0].astype(jnp.float32)
    grad_inputs, grad_first_gain, grad_first_up, grad_first_down = feed_back(
        grad_first_out, inputs, first_gains[0], first_back[1], first_back[2], first_kept
    )
    zero_row = jnp.zeros_like(grad_first_gain)
    grad_rows = jnp.stack(
        [
            grad_first_gain,
            grad_attend_gain,
            bias_sums[0],
            bias_sums[1],
            grad_conv_gain,
            zero_row,
            zero_row,
            grad_second_gain,
            grad_final_gain,
        ]
    )
    first_shards = (
        lax.psum_scatter(
            grad_rows.astype(jnp.bfloat16), "shard", scatter_dimension=1, tiled=True
        ).astype(jnp.float32),
        lax.psum_scatter(
            grad_first_up.astype(jnp.bfloat16), "shard", scatter_dimension=0, tiled=True
        ).astype(jnp.float32),
        lax.psum_scatter(
            grad_first_down.astype(jnp.bfloat16), "shard", scatter_dimension=0, tiled=True
        ).astype(jnp.float32),
    )
    summed = (
        lax.psum(first_shards[0].astype(jnp.bfloat16), "replica").astype(jnp.float32),
        lax.psum(first_shards[1].astype(jnp.bfloat16), "replica").astype(jnp.float32),
        lax.psum(first_shards[2].astype(jnp.bfloat16), "replica").astype(jnp.float32),
        lax.psum(attend_shards[0].astype(jnp.bfloat16), "replica").astype(jnp.float32),
        lax.psum(attend_shards[1].astype(jnp.bfloat16), "replica").astype(jnp.float32),
        lax.psum(attend_shards[2].astype(jnp.bfloat16), "replica").astype(jnp.float32),
        lax.psum(conv_shards[0].astype(jnp.bfloat16), "replica").astype(jnp.float32),
        lax.psum(conv_shards[1].astype(jnp.bfloat16), "replica").astype(jnp.float32),
        lax.psum(conv_shards[2].astype(jnp.bfloat16), "replica").astype(jnp.float32),
        lax.psum(second_shards[0].astype(jnp.bfloat16), "replica").astype(jnp.float32),
        lax.psum(second_shards[1].astype(jnp.bfloat16), "replica").astype(jnp.float32),
    )
    shard_cols = summed[0].shape[1]
    first_col = lax.axis_index("shard") * shard_cols
    gain_part = lax.dynamic_slice_in_dim(gain_total, first_col, shard_cols)
    shift_part = lax.dynamic_slice_in_dim(shift_total, first_col, shard_cols)
    grad_vectors = summed[0].at[5].add(gain_part).at[6].add(shift_part)
    return (
        output.astype(jnp.bfloat16).reshape(clip_count, clip_length, model_width),
        grad_inputs.astype(jnp.bfloat16).reshape(clip_count, clip_length, model_width),
        grad_vectors,
        summed[1],
        summed[2],
        summed[3],
        summed[4],
        summed[5],
        summed[6],
        summed[7],
        summed[8],
        summed[9],
        summed[10],
    )


def solution(mesh):
    return jax.shard_map(
        body,
        mesh=mesh,
        in_specs=(
            P(("replica", "shard"), None, None),
            P(("replica", "shard"), None),
            P(("replica", "shard"), None, None),
            P(None, "shard"),
            P("shard", None),
            P("shard", None),
            P("shard", None),
            P("shard", None),
            P("shard", None),
            P("shard", None),
            P(None, "shard"),
            P("shard", None),
            P("shard", None),
            P("shard", None),
        ),
        out_specs=(
            P(("replica", "shard"), None, None),
            P(("replica", "shard"), None, None),
            P(None, "shard"),
            P("shard", None),
            P("shard", None),
            P("shard", None),
            P("shard", None),
            P("shard", None),
            P("shard", None),
            P(None, "shard"),
            P("shard", None),
            P("shard", None),
            P("shard", None),
        ),
        check_vma=False,
    )
```

profile of v0, /device:TPU:0, one launch (start us, length us, event | category | flops | bytes accessed | tf_op | source)
XLA Modules:
  0.0 1763.8 jit_solution(10845078142952781620)
XLA Ops:
  13.5 43.3 %all_gather.50 = bf16[31,512]{0,1:T(8,128)(2,1)S(1)} all-gather(bf16[31,32]{0,1:T(8,128)(2,1)S(1)} %copy.87), channel_id=1, replica_groups=mesh['replica'=2,'shard'=16] {'shard'}, dimensions={1}, use_global_device_ids=true | all-gather | bytes 33728 | tf_op jit(solution)/shard_map/all_gather | solution.py:225
  62.4 36.2 %all-gather = bf16[16,32,9]{1,2,0:T(8,128)(2,1)S(1)} all-gather(bf16[1,32,9]{1,2,0:T(8,128)(2,1)S(1)} %bitcast.357), channel_id=1, replica_groups=mesh['replica'=2,'shard'=16] {'shard'}, dimensions={0}, use_global_device_ids=true | all-gather | bytes 9792 | tf_op jit(solution)/shard_map/all_gather | solution.py:210
  99.5 43.0 %all_gather.48 = bf16[512,512]{1,0:T(8,128)(2,1)S(1)} all-gather(bf16[32,512]{1,0:T(8,128)(2,1)S(1)} %copy-done.75), channel_id=1, replica_groups=mesh['replica'=2,'shard'=16] {'shard'}, dimensions={0}, use_global_device_ids=true | all-gather | bytes 557056 | tf_op jit(solution)/shard_map/all_gather | solution.py:218
  143.5 42.6 %all_gather.49 = bf16[512,512]{1,0:T(8,128)(2,1)} all-gather(bf16[32,512]{1,0:T(8,128)(2,1)S(1)} %copy-done.76), channel_id=1, replica_groups=mesh['replica'=2,'shard'=16] {'shard'}, dimensions={0}, use_global_device_ids=true | all-gather | bytes 557056 | tf_op jit(solution)/shard_map/all_gather | solution.py:219
  186.1 43.9 %all_gather.52 = bf16[512,512]{1,0:T(8,128)(2,1)} all-gather(bf16[32,512]{1,0:T(8,128)(2,1)S(1)} %copy-done.77), channel_id=1, replica_groups=mesh['replica'=2,'shard'=16] {'shard'}, dimensions={0}, use_global_device_ids=true | all-gather | bytes 557056 | tf_op jit(solution)/shard_map/all_gather | solution.py:226
  230.5 8.5 multiply_convert_fusion.2
  245.1 6.4 fusion.89
  251.6 8.0 copy.85
  259.6 40.7 %while.31 = (s32[]{:T(128)}, bf16[2,544,512]{2,1,0:T(8,128)(2,1)}, f32[2,8,544,1]{2,1,3,0:T(8,128)S(1)}, f32[2,544,1536]{1,2,0:T(8,128)}, f32[9,512]{1,0:T(8,128...) while((s32[]{:T(128)}, bf16[2,544,512]{2,1,0:T(8,128)(2,1)}, ...), condition=%wide.region_7.8_spmd, body=%wide.region_4.7_spmd.sunk | while | flops 3353752064 | bytes 107094576 | solution.py:249
  309.0 9.8 fusion.99
  318.8 37.2 %psum.105 = f32[512]{0:T(512)S(1)} all-reduce(f32[512]{0:T(512)S(1)} %get-tuple-element.456), channel_id=1, replica_groups=mesh['replica'=2,'shard'=16] {'replica','shard'}, use_global_device_ids=true, to_apply=%region_11.12 | all-reduce | flops 512 | bytes 4096 | tf_op jit(solution)/shard_map/psum | solution.py:260
  356.3 41.5 %psum.106 = f32[512]{0:T(512)S(1)} all-reduce(f32[512]{0:T(512)S(1)} %multiply_reduce_fusion.43), channel_id=1, replica_groups=mesh['replica'=2,'shard'=16] {'replica','shard'}, use_global_device_ids=true, to_apply=%region_13.14 | all-reduce | flops 512 | bytes 4096 | tf_op jit(solution)/shard_map/psum | solution.py:262
  403.3 10.2 multiply_convert_fusion.1
  413.5 6.1 fusion.113
  426.5 7.7 fusion.65
  443.9 39.9 %all-reduce.65 = (f32[512]{0:T(512)S(1)}, f32[512]{0:T(512)S(1)}) all-reduce(f32[512]{0:T(512)S(1)} %get-tuple-element.361, f32[512]{0:T(512)S(1)} %get-tuple-element.360), channel_id=1, replica_groups=mesh['replica'=2,'shard'=16] {'replica','shard'}, use_global_device_ids=true, to_apply=%region_25.26 | all-reduce | flops 1024 | bytes 8192 | tf_op jit(solution)/shard_map/psum | solution.py:291
  486.0 13.2 broadcast_multiply_fusion
  499.2 6.3 broadcast_multiply_fusion.1
  505.5 6.5 multiply_reduce_fusion.30
  517.6 20.7 %pad_add_fusion = f32[2,574,512]{2,1,0:T(8,128)S(1)} fusion(f32[2,544,512]{2,1,0:T(8,128)} %get-tuple-element.501, f32[2,544,512]{2,1,0:T(8,128)} %get-tuple-element.502, f32[2,544,512]{2,1,0:T(8,128)} %get-tuple-element.503, f32[2,544,512]{2,1,0:T(8,128)} %get-tuple-element.504, f32[2,544,512]{2,1,0:T(8,128)} %get-tuple-element.505, ...), kind=kLoop, calls=%fused_computation.117 | loop fusion | flops 14106624 | bytes 58056704 | tf_op jit(solution)/shard_map/transpose(jvp())/add_any | solution.py:51
  538.3 7.8 fusion.73
  558.6 220.1 %while.32 = (s32[]{:T(128)}, f32[512]{0:T(512)}, f32[512]{0:T(512)}, f32[512,8,64]{0,2,1:T(8,128)}, bf16[2,544,1536]{2,1,0:T(8,128)(2,1)}, /*index=5*/f32[2,544,...) while((s32[]{:T(128)}, f32[512]{0:T(512)}, ...), condition=%wide.region_32.33_spmd.clone, body=%wide.region_28.32_spmd.clone.sunk | while | flops 7341285888 | bytes 249963088 | solution.py:340
  580.9 6.8 fusion.248
  587.7 18.4 %fusion.251 = (f32[8,64]{1,0:T(8,128)}, f32[544,8,64]{0,2,1:T(8,128)}) fusion(bf16[544,8,64]{0,2,1:T(8,128)(2,1)} %bitcast.266, f32[8,544,544]{1,2,0:T(8,128)} %subtract_exponential_fusion.2, f32[8,544,544]{1,2,0:T(8,128)} %fusion.248), kind=kOutput, calls=%fused_computation.317.clone.1 | convolution fusion | flops 322261280 | bytes 20613120 | tf_op jit(solution)/shard_map/while/body/eval_jaxpr/hij,jhd->ihd/dot_general | solution.py:153
  606.2 20.7 %fusion.249 = f32[8,544,512]{2,1,0:T(8,128)} fusion(f32[8,544,544]{1,2,0:T(8,128)} %subtract_exponential_fusion.2, f32[8,544,544]{1,2,0:T(8,128)} %fusion.248, bf16[544,256]{1,0:T(8,128)(2,1)} %copy-done.28, bf16[544,256]{1,0:T(8,128)(2,1)S(1)} %get-tuple-element.730), kind=kOutput, calls=%fused_computation.46.clone.1 | convolution fusion | flops 2444366592 | bytes 28409856 | tf_op jit(solution)/shard_map/while/body/eval_jaxpr/hij,je->hie/dot_general | solution.py:157
  635.3 17.4 fusion.254
  690.7 6.8 fusion.248
  697.5 18.4 %fusion.251 = (f32[8,64]{1,0:T(8,128)}, f32[544,8,64]{0,2,1:T(8,128)}) fusion(bf16[544,8,64]{0,2,1:T(8,128)(2,1)} %bitcast.266, f32[8,544,544]{1,2,0:T(8,128)} %subtract_exponential_fusion.2, f32[8,544,544]{1,2,0:T(8,128)} %fusion.248), kind=kOutput, calls=%fused_computation.317.clone.1 | convolution fusion | flops 322261280 | bytes 20613120 | tf_op jit(solution)/shard_map/while/body/eval_jaxpr/hij,jhd->ihd/dot_general | solution.py:153
  715.9 20.7 %fusion.249 = f32[8,544,512]{2,1,0:T(8,128)} fusion(f32[8,544,544]{1,2,0:T(8,128)} %subtract_exponential_fusion.2, f32[8,544,544]{1,2,0:T(8,128)} %fusion.248, bf16[544,256]{1,0:T(8,128)(2,1)} %copy-done.28, bf16[544,256]{1,0:T(8,128)(2,1)S(1)} %get-tuple-element.730), kind=kOutput, calls=%fused_computation.46.clone.1 | convolution fusion | flops 2444366592 | bytes 28409856 | tf_op jit(solution)/shard_map/while/body/eval_jaxpr/hij,je->hie/dot_general | solution.py:157
  745.1 17.4 fusion.254
  793.1 7.3 multiply_reduce_fusion.35
  828.8 7.5 convolution_convert_fusion.1
  836.4 6.9 convolution_convert_fusion
  843.4 7.4 convolution_convert_fusion.3
  850.9 6.4 convolution_convert_fusion.4
  859.8 20.4 %reduce-scatter.34.cloned.1.call-done = bf16[32,9]{1,0:T(8,128)(2,1)} async-done(((bf16[512,9]{1,0:T(8,128)(2,1)}), bf16[32,9]{1,0:T(8,128)(2,1)}) %reduce-scatter.34.cloned.1.call-update) | async-done | bytes 592
  881.5 73.7 %reduce-scatter.38.cloned.1.call-done = bf16[32,31]{1,0:T(8,128)(2,1)} async-done(((bf16[512,31]{1,0:T(8,128)(2,1)}), bf16[32,31]{1,0:T(8,128)(2,1)}) %reduce-scatter.38.cloned.1.call-update) | async-done | bytes 2000
  956.6 73.8 %reduce-scatter.36.cloned.1.call-done = bf16[32,512]{1,0:T(8,128)(2,1)} async-done(((bf16[512,512]{1,0:T(8,128)(2,1)}), bf16[32,512]{1,0:T(8,128)(2,1)}) %reduce-scatter.36.cloned.1.call-update) | async-done | bytes 32784
  1031.9 73.6 %reduce-scatter.24.cloned.1.call-done = bf16[32,512]{1,0:T(8,128)(2,1)} async-done(((bf16[512,512]{1,0:T(8,128)(2,1)}), bf16[32,512]{1,0:T(8,128)(2,1)}) %reduce-scatter.24.cloned.1.call-update) | async-done | bytes 32784 | tf_op jit(solution)/shard_map/reduce_scatter | solution.py:357
  1105.6 75.2 %reduce-scatter.28.cloned.1.call-done = bf16[32,512]{1,0:T(8,128)(2,1)} async-done(((bf16[512,512]{1,0:T(8,128)(2,1)}), bf16[32,512]{1,0:T(8,128)(2,1)}) %reduce-scatter.28.cloned.1.call-update) | async-done | bytes 32784 | tf_op jit(solution)/shard_map/reduce_scatter | solution.py:315
  1180.9 76.8 %reduce-scatter.26.cloned.1.call-done = bf16[32,1024]{1,0:T(8,128)(2,1)} async-done(((bf16[512,1024]{1,0:T(8,128)(2,1)}), bf16[32,1024]{1,0:T(8,128)(2,1)}) %reduce-scatter.26.cloned.1.call-update) | async-done | bytes 65552 | tf_op jit(solution)/shard_map/reduce_scatter | solution.py:309
  1257.7 125.9 %reduce-scatter.22.cloned.1.call-done = bf16[32,1536]{1,0:T(8,128)(2,1)} async-done(((bf16[512,1536]{1,0:T(8,128)(2,1)}), bf16[32,1536]{1,0:T(8,128)(2,1)}) %reduce-scatter.22.cloned.1.call-update) | async-done | bytes 98320 | tf_op jit(solution)/shard_map/reduce_scatter | solution.py:351
  1383.5 81.9 %reduce-scatter.30.cloned.1.call-done = bf16[32,2048]{1,0:T(8,128)(2,1)} async-done(((bf16[512,2048]{1,0:T(8,128)(2,1)}), bf16[32,2048]{1,0:T(8,128)(2,1)}) %reduce-scatter.30.cloned.1.call-update) | async-done | bytes 131088 | tf_op jit(solution)/shard_map/reduce_scatter | solution.py:280
  1465.4 79.5 %reduce-scatter.32.cloned.1.call-done = bf16[128,512]{1,0:T(8,128)(2,1)} async-done(((bf16[2048,512]{1,0:T(8,128)(2,1)}), bf16[128,512]{1,0:T(8,128)(2,1)}) %reduce-scatter.32.cloned.1.call-update) | async-done | bytes 131088 | tf_op jit(solution)/shard_map/reduce_scatter | solution.py:283
  1544.9 79.9 %reduce-scatter.20.cloned.1.call-done = bf16[128,512]{1,0:T(8,128)(2,1)} async-done(((bf16[2048,512]{1,0:T(8,128)(2,1)}), bf16[128,512]{1,0:T(8,128)(2,1)}) %reduce-scatter.20.cloned.1.call-update) | async-done | bytes 131088 | tf_op jit(solution)/shard_map/reduce_scatter | solution.py:387
  1624.7 80.0 %reduce-scatter.18.cloned.1.call-done = bf16[32,2048]{1,0:T(8,128)(2,1)} async-done(((bf16[512,2048]{1,0:T(8,128)(2,1)}), bf16[32,2048]{1,0:T(8,128)(2,1)}) %reduce-scatter.18.cloned.1.call-update) | async-done | bytes 131088 | tf_op jit(solution)/shard_map/reduce_scatter | solution.py:384
  1707.6 16.6 all-reduce.71.cloned.1.call-done
  1732.1 15.4 all-reduce.73.cloned.1.call-done
  (619 shorter events, 272.0 us)
Async XLA Ops:
  7.2 223.3 %all-gather.8.cloned.1.call-start = ((), (), s32[]{:S(2)}) async-start(), calls=%async_computation.11 | async-start | bytes 2228224 | tf_op jit(solution)/shard_map/all_gather | solution.py:211
  7.9 231.0 %all-gather.10.cloned.1.call-start = ((), (), s32[]{:S(2)}) async-start(), calls=%async_computation.12 | async-start | bytes 2228224 | tf_op jit(solution)/shard_map/all_gather | solution.py:212
  8.7 236.4 %all-gather.12.cloned.1.call-start = ((), (), s32[]{:S(2)}) async-start(), calls=%async_computation.13 | async-start | bytes 1671168 | tf_op jit(solution)/shard_map/all_gather | solution.py:217
  9.4 294.4 %all-gather.14.cloned.1.call-start = ((), (), s32[]{:S(2)}) async-start(), calls=%async_computation.14 | async-start | bytes 1114112 | tf_op jit(solution)/shard_map/all_gather | solution.py:224
  10.0 393.3 %all-gather.16.cloned.1.call-start = ((), (), s32[]{:S(2)}) async-start(), calls=%async_computation.15 | async-start | bytes 2228224 | tf_op jit(solution)/shard_map/all_gather | solution.py:231
  10.6 402.9 %all-gather.18.cloned.1.call-start = ((), (), s32[]{:S(2)}) async-start(), calls=%async_computation.16 | async-start | bytes 2228224 | tf_op jit(solution)/shard_map/all_gather | solution.py:232
  11.2 869.0 %reduce-scatter.34.cloned.1.call-start = ((), (), s32[]{:S(2)}) async-start(), calls=%async_computation.25 | async-start | bytes 139264
  13.4 216.6 %copy-start.55 = (f32[1088]{0:T(1024)}, f32[1088]{0:T(1024)S(1)}, u32[]{:S(2)}) copy-start(f32[1088]{0:T(1024)S(1)} %div.131) | copy-start | bytes 13060
  60.1 39.4 %copy-start.75 = (bf16[32,512]{1,0:T(8,128)(2,1)S(1)}, bf16[32,512]{1,0:T(8,128)(2,1)}, u32[]{:S(2)}) copy-start(bf16[32,512]{1,0:T(8,128)(2,1)} %param.29) | copy-start | bytes 98308
  60.1 83.4 %copy-start.76 = (bf16[32,512]{1,0:T(8,128)(2,1)S(1)}, bf16[32,512]{1,0:T(8,128)(2,1)}, u32[]{:S(2)}) copy-start(bf16[32,512]{1,0:T(8,128)(2,1)} %param.30) | copy-start | bytes 98308
  60.1 126.1 %copy-start.77 = (bf16[32,512]{1,0:T(8,128)(2,1)S(1)}, bf16[32,512]{1,0:T(8,128)(2,1)}, u32[]{:S(2)}) copy-start(bf16[32,512]{1,0:T(8,128)(2,1)} %param.33) | copy-start | bytes 98308
  99.4 131.1 %copy-start.78 = (f32[1,512]{1,0:T(1,128)}, f32[1,512]{1,0:T(1,128)S(1)}, u32[]{:S(2)}) copy-start(f32[1,512]{1,0:T(1,128)S(1)} %get-tuple-element.531) | copy-start | bytes 6148
  99.4 145.7 %copy-start.67 = (f32[1,512]{1,0:T(1,128)}, f32[1,512]{1,0:T(1,128)S(1)}, u32[]{:S(2)}) copy-start(f32[1,512]{1,0:T(1,128)S(1)} %get-tuple-element.530) | copy-start | bytes 6148
  99.5 131.0 %copy-start.65 = (f32[1088]{0:T(1024)}, f32[1088]{0:T(1024)S(1)}, u32[]{:S(2)}) copy-start(f32[1088]{0:T(1024)S(1)} %add.505) | copy-start | bytes 13060
  99.5 131.0 %copy-start.49 = (f32[1088]{0:T(1024)}, f32[1088]{0:T(1024)S(1)}, u32[]{:S(2)}) copy-start(f32[1088]{0:T(1024)S(1)} %rsqrt.58) | copy-start | bytes 13060
  303.3 250.2 %copy-start.53 = (f32[1088]{0:T(1024)}, f32[1088]{0:T(1024)S(1)}, u32[]{:S(2)}) copy-start(f32[1088]{0:T(1024)S(1)} %broadcast_multiply_fusion.33) | copy-start | bytes 13060
  303.8 249.7 %copy-start.71 = (f32[1088]{0:T(1024)}, f32[1088]{0:T(1024)S(1)}, u32[]{:S(2)}) copy-start(f32[1088]{0:T(1024)S(1)} %fusion.83) | copy-start | bytes 13060
  318.8 79.0 %copy-start.148 = (f32[1,512]{1,0:T(1,128)S(1)}, f32[1,512]{1,0:T(1,128)}, u32[]{:S(2)}) copy-start(f32[1,512]{1,0:T(1,128)} %get-tuple-element.528) | copy-start | bytes 6148
  401.4 36.4 %copy-start.51 = (f32[1088]{0:T(1024)}, f32[1088]{0:T(1024)S(1)}, u32[]{:S(2)}) copy-start(f32[1088]{0:T(1024)S(1)} %broadcast_multiply_fusion.32) | copy-start | bytes 13060
  403.2 34.6 %copy-start.69 = (f32[1088]{0:T(1024)}, f32[1088]{0:T(1024)S(1)}, u32[]{:S(2)}) copy-start(f32[1088]{0:T(1024)S(1)} %fusion.84) | copy-start | bytes 13060
  426.5 12.3 copy-start.73
  792.8 11.7 copy-start.113
  792.8 11.7 copy-start.114
  792.8 11.7 copy-start.115
  792.8 11.7 copy-start.116
  792.9 11.7 copy-start.117
  792.9 11.7 copy-start.118
  792.9 11.7 copy-start.119
  792.9 11.7 copy-start.120
  792.9 11.7 copy-start.121
  792.9 11.7 copy-start.122
  792.9 11.7 copy-start.123
  792.9 11.7 copy-start.124
  792.9 11.7 copy-start.125
  792.9 11.7 copy-start.126
  804.5 150.8 %reduce-scatter.38.cloned.1.call-start = ((), (), s32[]{:S(2)}) async-start(), calls=%async_computation.27 | async-start | bytes 139264
  805.8 224.6 %reduce-scatter.36.cloned.1.call-start = ((), (), s32[]{:S(2)}) async-start(), calls=%async_computation.26 | async-start | bytes 557056
  810.0 295.6 %reduce-scatter.24.cloned.1.call-start = ((), (), s32[]{:S(2)}) async-start(), calls=%async_computation.20 | async-start | bytes 557056 | tf_op jit(solution)/shard_map/reduce_scatter | solution.py:357
  813.8 367.0 %reduce-scatter.28.cloned.1.call-start = ((), (), s32[]{:S(2)}) async-start(), calls=%async_computation.22 | async-start | bytes 557056 | tf_op jit(solution)/shard_map/reduce_scatter | solution.py:315
  817.9 439.8 %reduce-scatter.26.cloned.1.call-start = ((), (), s32[]{:S(2)}) async-start(), calls=%async_computation.21 | async-start | bytes 1114112 | tf_op jit(solution)/shard_map/reduce_scatter | solution.py:309
  823.0 560.6 %reduce-scatter.22.cloned.1.call-start = ((), (), s32[]{:S(2)}) async-start(), calls=%async_computation.19 | async-start | bytes 1671168 | tf_op jit(solution)/shard_map/reduce_scatter | solution.py:351
  828.7 636.7 %reduce-scatter.30.cloned.1.call-start = ((), (), s32[]{:S(2)}) async-start(), calls=%async_computation.23 | async-start | bytes 2228224 | tf_op jit(solution)/shard_map/reduce_scatter | solution.py:280
  836.3 708.6 %reduce-scatter.32.cloned.1.call-start = ((), (), s32[]{:S(2)}) async-start(), calls=%async_computation.24 | async-start | bytes 2228224 | tf_op jit(solution)/shard_map/reduce_scatter | solution.py:283
  843.3 781.4 %reduce-scatter.20.cloned.1.call-start = ((), (), s32[]{:S(2)}) async-start(), calls=%async_computation.18 | async-start | bytes 2228224 | tf_op jit(solution)/shard_map/reduce_scatter | solution.py:387
  850.8 853.9 %reduce-scatter.18.cloned.1.call-start = ((), (), s32[]{:S(2)}) async-start(), calls=%async_computation.17 | async-start | bytes 2228224 | tf_op jit(solution)/shard_map/reduce_scatter | solution.py:384
  857.2 866.9 %all-reduce.71.cloned.1.call-start = ((), (), s32[]{:S(2)}) async-start(), calls=%async_computation.28 | async-start | bytes 417792 | tf_op jit(solution)/shard_map/psum | solution.py:396
  1180.8 566.7 %all-reduce.73.cloned.1.call-start = ((), (), s32[]{:S(2)}) async-start(), calls=%async_computation.29 | async-start | bytes 1376256 | tf_op jit(solution)/shard_map/psum | solution.py:393
  1732.1 25.0 %copy-start.112 = (f32[9,32]{1,0:T(8,128)}, f32[9,32]{1,0:T(8,128)S(1)}, u32[]{:S(2)}) copy-start(f32[9,32]{1,0:T(8,128)S(1)} %scatter-add.9) | copy-start | bytes 3460
  (160 other events, 721.2 us)
Sparse Core Ops, SparseCore 0:
  10.8 64.3 all-gather.7
  78.0 62.6 all-gather.9
  143.4 60.8 all-gather.11
  206.9 53.9 all-gather.13
  263.6 59.5 all-gather.15
  325.8 60.5 all-gather.17
  804.6 75.5 reduce-scatter.33
  883.1 72.1 reduce-scatter.37
  957.5 72.8 reduce-scatter.35
  1032.6 72.9 reduce-scatter.23
  1107.8 72.9 reduce-scatter.27
  1183.6 74.0 reduce-scatter.25
  1262.5 121.0 reduce-scatter.21
  1385.7 79.6 reduce-scatter.29
  1467.5 77.2 reduce-scatter.31
  1547.0 77.7 reduce-scatter.19
  1626.9 77.7 reduce-scatter.17
  1708.3 15.7 all-reduce.70
  1726.9 20.4 all-reduce.72
where the time goes:
time: 1770 us; the launch traced here: 1760 us
  waiting for transfers between devices  876 us (49%)
  blocking collectives  328 us (19%)
  matrix products  317 us (18%)
  other arithmetic  156 us (9%)
  local copies, waits for them, and re-layouts  67.9 us (4%)
    unnamed x22, waiting for transfers between devices  172 us
    reduce_scatter x1, waiting for transfers between devices, body(): lax.psum_scatter(grad_qkv.astype(jnp.bfloat16), 'shard', scatter_dimensio...  126 us
    reduce_scatter x1, waiting for transfers between devices, body(): lax.psum_scatter(grad_second_up.astype(jnp.bfloat16), 'shard', scatter_di...  81.9 us
    reduce_scatter x1, waiting for transfers between devices, body(): lax.psum_scatter(grad_first_up.astype(jnp.bfloat16), 'shard', scatter_dim...  80 us
    reduce_scatter x1, waiting for transfers between devices, body(): lax.psum_scatter(grad_first_down.astype(jnp.bfloat16), 'shard', scatter_d...  79.9 us
    reduce_scatter x1, waiting for transfers between devices, body(): lax.psum_scatter(grad_second_down.astype(jnp.bfloat16), 'shard', scatter_...  79.5 us
    reduce_scatter x1, waiting for transfers between devices, body(): lax.psum_scatter(grad_point_glu.astype(jnp.bfloat16), 'shard', scatter_di...  76.8 us
    reduce_scatter x1, waiting for transfers between devices, body(): lax.psum_scatter(grad_point_out.astype(jnp.bfloat16), 'shard', scatter_di...  75.2 us
  transfers between devices with their start and end apart: 19, of which 13 were waited for; matrix products, arithmetic and copies ran while one was open for 10% of the time, Pallas kernels for 0%

commit v1 on v0

--- a/solution.py
+++ b/solution.py
@@ -183,6 +183,31 @@
         jnp.sum(grad_query_v, axis=0).reshape(-1),
         grad_place,
     )
+
+
+def fold_down(rows, parts, depth):
+    blocks = rows.reshape(parts, -1, depth, rows.shape[-1])
+    return blocks.transpose(0, 2, 1, 3).reshape(parts * depth, -1)
+
+
+def unfold_down(block, parts, width):
+    depth = block.shape[0] // parts
+    pieces = block.reshape(parts, depth, -1, width)
+    return pieces.transpose(0, 2, 1, 3).reshape(-1, width)
+
+
+def pack_small(columns):
+    joined = jnp.concatenate(columns, axis=1)
+    return jnp.pad(joined, ((0, 0), (0, -joined.shape[1] % 128)))
+
+
+def split_columns(block, widths):
+    pieces = []
+    start = 0
+    for width in widths:
+        pieces.append(block[:, start : start + width])
+        start += width
+    return pieces
 
 
 def body(
@@ -205,39 +230,46 @@
     row_count = clip_count * clip_length
     token_count = row_count * lax.axis_size("replica") * lax.axis_size("shard")
 
-    def first_block():
-        return (
-            lax.all_gather(vectors, "shard", axis=1, tiled=True),
-            lax.all_gather(first_up, "shard", axis=0, tiled=True),
-            lax.all_gather(first_down, "shard", axis=0, tiled=True),
-        )
-
-    def attend_block():
-        return (
-            lax.all_gather(query_key_value, "shard", axis=0, tiled=True),
-            lax.all_gather(place_weight, "shard", axis=0, tiled=True),
-            lax.all_gather(out_weight, "shard", axis=0, tiled=True),
-        )
-
-    def conv_block():
-        return (
-            lax.all_gather(point_glu, "shard", axis=0, tiled=True),
-            lax.all_gather(depth_taps, "shard", axis=1, tiled=True),
-            lax.all_gather(point_out, "shard", axis=0, tiled=True),
-        )
-
-    def second_block():
-        return (
-            lax.all_gather(second_up, "shard", axis=0, tiled=True),
-            lax.all_gather(second_down, "shard", axis=0, tiled=True),
-        )
-
-    first_full = first_block()
+    shards = lax.axis_size("shard")
+    depth = first_up.shape[0]
+    hidden_width = first_up.shape[1]
+    row_total = vectors.shape[0]
+    tap_total = depth_taps.shape[0]
+
+    early = jnp.concatenate(
+        [
+            first_up,
+            fold_down(first_down, 1, depth),
+            query_key_value,
+            place_weight,
+            out_weight,
+            pack_small([vectors.T, depth_taps.T]),
+        ],
+        axis=1,
+    )
+    late = jnp.concatenate(
+        [point_glu, point_out, second_up, fold_down(second_down, 1, depth)], axis=1
+    )
+    early_full = lax.all_gather(early, "shard", axis=0, tiled=True)
+    late_full = lax.all_gather(late, "shard", axis=0, tiled=True)
+    pieces = split_columns(
+        early_full,
+        (hidden_width, hidden_width, 3 * model_width, model_width, model_width, 128),
+    )
+    small = pieces[5].T
+    first_full = (
+        small[:row_total],
+        pieces[0],
+        unfold_down(pieces[1], shards, model_width),
+    )
+    attend_full = (pieces[2], pieces[3], pieces[4])
+    pieces = split_columns(late_full, (2 * model_width, model_width, hidden_width, hidden_width))
+    conv_full = (pieces[0], small[row_total : row_total + tap_total], pieces[1])
+    second_full = (pieces[2], unfold_down(pieces[3], shards, model_width))
     gains = first_full[0].astype(jnp.float32)
     inputs = features.reshape(row_count, model_width).astype(jnp.float32)
     first_out, first_kept = feed_forward(inputs, gains[0], first_full[1], first_full[2])
     after_first = inputs + 0.5 * first_out
-    attend_full = attend_block()
     normed_attend = normalize(after_first, gains[1]).astype(jnp.bfloat16)
     joint_rows = product(normed_attend, attend_full[0])
     joint_clips = joint_rows.reshape(clip_count, clip_length, 3 * model_width)
@@ -249,7 +281,6 @@
     context_clips, logsum_clips = lax.map(forward_clip, (joint_clips, frame_times))
     context_low = context_clips.reshape(row_count, model_width)
     after_attend = after_first + product(context_low, attend_full[2])
-    conv_full = conv_block()
     normed_conv = normalize(after_attend, gains[4]).astype(jnp.bfloat16)
     mixed_rows = product(normed_conv, conv_full[0]).reshape(
         clip_count, clip_length, 2 * model_width
@@ -265,26 +296,17 @@
     shaped = unit_values * gains[5] + gains[6]
     active_conv = swish_act(shaped).astype(jnp.bfloat16)
     after_conv = after_attend + product(active_conv, conv_full[2])
-    second_full = second_block()
     second_out, second_kept = feed_forward(after_conv, gains[7], second_full[0], second_full[1])
     after_second = after_conv + 0.5 * second_out
     output = normalize(after_second, gains[8])
     grad_last, grad_final_gain = normalize_back(
         after_second, gains[8], cotangent.reshape(row_count, model_width).astype(jnp.float32)
     )
-    second_back = second_block()
+    second_back = second_full
     grad_conv_out, grad_second_gain, grad_second_up, grad_second_down = feed_back(
         grad_last, after_conv, gains[7], second_back[0], second_back[1], second_kept
     )
-    second_shards = (
-        lax.psum_scatter(
-            grad_second_up.astype(jnp.bfloat16), "shard", scatter_dimension=0, tiled=True
-        ).astype(jnp.float32),
-        lax.psum_scatter(
-            grad_second_down.astype(jnp.bfloat16), "shard", scatter_dimension=0, tiled=True
-        ).astype(jnp.float32),
-    )
-    conv_back = conv_block()
+    conv_back = conv_full
     grad_low = grad_conv_out.astype(jnp.bfloat16)
     grad_point_out = product_left(active_conv, grad_low)
     grad_shaped = product_right(grad_low, conv_back[2]) * swish_slope(shaped)
@@ -305,18 +327,19 @@
         after_attend, gains[4], product_right(grad_mixed_low, conv_back[0])
     )
     grad_attend_out = grad_conv_out + grad_extra
-    conv_shards = (
-        lax.psum_scatter(
-            grad_point_glu.astype(jnp.bfloat16), "shard", scatter_dimension=0, tiled=True
-        ).astype(jnp.float32),
-        lax.psum_scatter(
-            grad_taps.astype(jnp.bfloat16), "shard", scatter_dimension=1, tiled=True
-        ).astype(jnp.float32),
-        lax.psum_scatter(
-            grad_point_out.astype(jnp.bfloat16), "shard", scatter_dimension=0, tiled=True
-        ).astype(jnp.float32),
-    )
-    attend_back = attend_block()
+    late_grads = jnp.concatenate(
+        [
+            grad_point_glu.astype(jnp.bfloat16),
+            grad_point_out.astype(jnp.bfloat16),
+            grad_second_up.astype(jnp.bfloat16),
+            fold_down(grad_second_down.astype(jnp.bfloat16), shards, depth),
+            pack_small([grad_taps.T.astype(jnp.bfloat16)]),
+        ],
+        axis=1,
+    )
+    late_grads, grad_attend_out = lax.optimization_barrier((late_grads, grad_attend_out))
+    late_sums = lax.psum_scatter(late_grads, "shard", scatter_dimension=0, tiled=True)
+    attend_back = attend_full
     grad_low = grad_attend_out.astype(jnp.bfloat16)
     grad_out_weight = product_left(context_low, grad_low)
     grad_context = (
@@ -347,18 +370,7 @@
     )
     grad_first_out = grad_attend_out + grad_extra
     grad_place_full = bias_sums[2].reshape(model_width, model_width)
-    attend_shards = (
-        lax.psum_scatter(
-            grad_qkv.astype(jnp.bfloat16), "shard", scatter_dimension=0, tiled=True
-        ).astype(jnp.float32),
-        lax.psum_scatter(
-            grad_place_full.astype(jnp.bfloat16), "shard", scatter_dimension=0, tiled=True
-        ).astype(jnp.float32),
-        lax.psum_scatter(
-            grad_out_weight.astype(jnp.bfloat16), "shard", scatter_dimension=0, tiled=True
-        ).astype(jnp.float32),
-    )
-    first_back = first_block()
+    first_back = first_full
     first_gains = first_back[0].astype(jnp.float32)
     grad_inputs, grad_first_gain, grad_first_up, grad_first_down = feed_back(
         grad_first_out, inputs, first_gains[0], first_back[1], first_back[2], first_kept
@@ -377,29 +389,39 @@
             grad_final_gain,
         ]
     )
-    first_shards = (
-        lax.psum_scatter(
-            grad_rows.astype(jnp.bfloat16), "shard", scatter_dimension=1, tiled=True
-        ).astype(jnp.float32),
-        lax.psum_scatter(
-            grad_first_up.astype(jnp.bfloat16), "shard", scatter_dimension=0, tiled=True
-        ).astype(jnp.float32),
-        lax.psum_scatter(
-            grad_first_down.astype(jnp.bfloat16), "shard", scatter_dimension=0, tiled=True
-        ).astype(jnp.float32),
+    early_grads = jnp.concatenate(
+        [
+            grad_first_up.astype(jnp.bfloat16),
+            fold_down(grad_first_down.astype(jnp.bfloat16), shards, depth),
+            grad_qkv.astype(jnp.bfloat16),
+            grad_place_full.astype(jnp.bfloat16),
+            grad_out_weight.astype(jnp.bfloat16),
+            pack_small([grad_rows.T.astype(jnp.bfloat16)]),
+        ],
+        axis=1,
+    )
+    early_sums = lax.psum_scatter(early_grads, "shard", scatter_dimension=0, tiled=True)
+    late_total = lax.psum(late_sums, "replica").astype(jnp.float32)
+    early_total = lax.psum(early_sums, "replica").astype(jnp.float32)
+    pieces = split_columns(
+        early_total,
+        (hidden_width, hidden_width, 3 * model_width, model_width, model_width, row_total),
+    )
+    late_pieces = split_columns(
+        late_total, (2 * model_width, model_width, hidden_width, hidden_width, tap_total)
     )
     summed = (
-        lax.psum(first_shards[0].astype(jnp.bfloat16), "replica").astype(jnp.float32),
-        lax.psum(first_shards[1].astype(jnp.bfloat16), "replica").astype(jnp.float32),
-        lax.psum(first_shards[2].astype(jnp.bfloat16), "replica").astype(jnp.float32),
-        lax.psum(attend_shards[0].astype(jnp.bfloat16), "replica").astype(jnp.float32),
-        lax.psum(attend_shards[1].astype(jnp.bfloat16), "replica").astype(jnp.float32),
-        lax.psum(attend_shards[2].astype(jnp.bfloat16), "replica").astype(jnp.float32),
-        lax.psum(conv_shards[0].astype(jnp.bfloat16), "replica").astype(jnp.float32),
-        lax.psum(conv_shards[1].astype(jnp.bfloat16), "replica").astype(jnp.float32),
-        lax.psum(conv_shards[2].astype(jnp.bfloat16), "replica").astype(jnp.float32),
-        lax.psum(second_shards[0].astype(jnp.bfloat16), "replica").astype(jnp.float32),
-        lax.psum(second_shards[1].astype(jnp.bfloat16), "replica").astype(jnp.float32),
+        pieces[5].T,
+        pieces[0],
+        unfold_down(pieces[1], 1, model_width),
+        pieces[2],
+        pieces[3],
+        pieces[4],
+        late_pieces[0],
+        late_pieces[4].T,
+        late_pieces[1],
+        late_pieces[2],
+        unfold_down(late_pieces[3], 1, model_width),
     )
     shard_cols = summed[0].shape[1]
     first_col = lax.axis_index("shard") * shard_cols

time: 1770 us -> 1090 us (0.62)
  waiting for transfers between devices: 876 us -> 348 us
  blocking collectives: 328 us -> 118 us
  local copies, waits for them, and re-layouts: 67.9 us -> 133 us
    reduce_scatter x8 -> x2, waiting for transfers between devices: 673 us -> 147 us  [the longest x1 147 us: body(): lax.psum_scatter(early_grads, 'shard', scatter_dimension=0, tiled=True)]
    all_gather x5 -> x0, blocking collectives: 209 us -> none  [the longest x1 43.9 us: conv_block(): lax.all_gather(point_out, 'shard', axis=0, tiled=True)]
    all_gather x6 -> x2, waiting for transfers between devices: 0.09 us -> 181 us  [the longest x1 93.3 us: body(): early_full = lax.all_gather(early, 'shard', axis=0, tiled=True)]
    unnamed x22 -> x5, waiting for transfers between devices: 172 us -> 0.08 us
    broadcast_in_dim x0 -> x31, local copies, waits for them, and re-layouts: none -> 24.5 us  [depthwise(): tap_weights[offset] * padded[:, offset:offset + clip_length]]
  transfers between devices with their start and end apart: 19 -> 5, of which waited for: 13 -> 4; matrix products, arithmetic and copies ran while one was open for 10% -> 27% of each run, Pallas kernels for 0% -> 0%
where the time goes in v1:
time: 1090 us; the launch traced here: 1080 us
  waiting for transfers between devices  348 us (32%)
  matrix products  314 us (29%)
  other arithmetic  144 us (13%)
  local copies, waits for them, and re-layouts  133 us (12%)
  blocking collectives  118 us (11%)
  between operations  16.3 us (1%)
    reduce_scatter x1, waiting for transfers between devices, body(): lax.psum_scatter(early_grads, 'shard', scatter_dimension=0, tiled=True)  147 us
    all_gather x1, waiting for transfers between devices, body(): early_full = lax.all_gather(early, 'shard', axis=0, tiled=True)  93.3 us
    all_gather x1, waiting for transfers between devices, body(): late_full = lax.all_gather(late, 'shard', axis=0, tiled=True)  88.1 us
    dot_general x8, matrix products, product(): return jnp.dot(left_side, right_side, preferred_element_type=jnp.float32)  44.5 us
    dot_general x8, matrix products, product_right(): lax.dot_general(left_side, right_side, (((1,), (1,)), ((), ())), preferre...  42.1 us
    dot_general x2, matrix products, clip_backward(): jnp.einsum('hij,je->hie', grad_scores, basis_low, preferred_element_type=...  41.3 us
    psum x1, blocking collectives, body(): lax.psum(jnp.sum(centered * centered, axis=0), ('replica', 'shard'))  40.8 us
    psum x1, blocking collectives, body(): lax.psum((jnp.sum(grad_shaped, axis=0), jnp.sum(grad_shaped * unit_values...  39.2 us
  transfers between devices with their start and end apart: 5, of which 4 were waited for; matrix products, arithmetic and copies ran while one was open for 27% of the time, Pallas kernels for 0%

profile of v1, /device:TPU:0, one launch (start us, length us, event | category | flops | bytes accessed | tf_op | source)
XLA Modules:
  0.0 1075.5 jit_solution(5616495947782707938)
XLA Ops:
  14.9 88.1 %all-gather.5.cloned.1.call-done = bf16[512,5632]{1,0:T(8,128)(2,1)} async-done(((bf16[32,5632]{1,0:T(8,128)(2,1)}), bf16[512,5632]{1,0:T(8,128)(2,1)}) %all-gather.5.cloned.1.call-update) | async-done | bytes 5767184 | tf_op jit(solution)/shard_map/all_gather | solution.py:254
  106.2 3.3 reshape.713
  111.4 93.3 %all-gather.3.cloned.1.call-done = bf16[512,6784]{1,0:T(8,128)(2,1)} async-done(((bf16[32,6784]{1,0:T(8,128)(2,1)}), bf16[512,6784]{1,0:T(8,128)(2,1)}) %all-gather.3.cloned.1.call-update) | async-done | bytes 6946832 | tf_op jit(solution)/shard_map/all_gather | solution.py:253
  215.1 3.3 reshape.704
  219.5 19.2 %multiply_convert_fusion.2 = (bf16[1088,2048]{1,0:T(8,128)(2,1)S(1)}, f32[1088,2048]{1,0:T(8,128)}) fusion(bf16[1088,512]{1,0:T(8,128)(2,1)S(1)} %multiply_convert_fusion.10, bf16[512,6784]{1,0:T(8,128)(2,1)} %all-gather.3.cloned.1.call-done), kind=kOutput, calls=%fused_computation.89 | convolution fusion | flops 2292842496 | bytes 16580608 | tf_op jit(solution)/shard_map/dot_general | solution.py:62
  244.2 4.8 fusion.92
  249.0 8.0 copy.260
  258.1 40.8 %while.31 = (s32[]{:T(128)}, bf16[2,544,512]{2,1,0:T(8,128)(2,1)}, f32[2,8,544,1]{2,1,3,0:T(8,128)S(1)}, f32[2,544,1536]{1,2,0:T(8,128)}, f32[9,512]{1,0:T(8,128...) while((s32[]{:T(128)}, bf16[2,544,512]{2,1,0:T(8,128)(2,1)}, ...), condition=%wide.region_7.8_spmd, body=%wide.region_4.7_spmd.sunk | while | flops 3353752064 | bytes 107094576 | solution.py:281
  308.2 9.8 fusion.125
  318.1 38.4 %psum.42 = f32[512]{0:T(512)S(1)} all-reduce(f32[512]{0:T(512)S(1)} %get-tuple-element.471), channel_id=1, replica_groups=mesh['replica'=2,'shard'=16] {'replica','shard'}, use_global_device_ids=true, to_apply=%region_11.12 | all-reduce | flops 512 | bytes 4096 | tf_op jit(solution)/shard_map/psum | solution.py:291
  356.8 40.8 %psum.43 = f32[512]{0:T(512)S(1)} all-reduce(f32[512]{0:T(512)S(1)} %multiply_reduce_fusion.43), channel_id=1, replica_groups=mesh['replica'=2,'shard'=16] {'replica','shard'}, use_global_device_ids=true, to_apply=%region_13.14 | all-reduce | flops 512 | bytes 4096 | tf_op jit(solution)/shard_map/psum | solution.py:293
  402.7 7.6 multiply_convert_fusion.1
  419.9 7.7 fusion.65
  427.6 6.8 multiply_reduce_fusion.1
  437.7 4.3 fusion.119
  442.0 39.2 %all-reduce.68 = (f32[512]{0:T(512)S(1)}, f32[512]{0:T(512)S(1)}) all-reduce(f32[512]{0:T(512)S(1)} %get-tuple-element.378, f32[512]{0:T(512)S(1)} %get-tuple-element.377), channel_id=1, replica_groups=mesh['replica'=2,'shard'=16] {'replica','shard'}, use_global_device_ids=true, to_apply=%region_25.26 | all-reduce | flops 1024 | bytes 8192 | tf_op jit(solution)/shard_map/psum | solution.py:313
  483.4 13.2 %broadcast_multiply_fusion = (f32[2,544,512]{2,1,0:T(8,128)}, f32[2,544,512]{2,1,0:T(8,128)}, f32[2,544,512]{2,1,0:T(8,128)}, f32[2,544,512]{2,1,0:T(8,128)}, f3...) fusion(f32[2,544,512]{2,1,0:T(8,128)S(1)} %bitcast.283, ...), kind=kLoop, calls=%fused_computation.217 | loop fusion | flops 10027008 | bytes 42373120 | tf_op jit(solution)/shard_map/transpose(jvp())/mul | solution.py:51
  496.6 7.7 broadcast_multiply_fusion.1
  504.3 5.8 multiply_reduce_fusion.37
  510.1 5.0 multiply_reduce_fusion.38
  515.2 4.7 convolution_convert_fusion.4
  521.8 20.8 %pad_add_fusion = f32[2,574,512]{2,1,0:T(8,128)S(1)} fusion(f32[2,544,512]{2,1,0:T(8,128)} %get-tuple-element.516, f32[2,544,512]{2,1,0:T(8,128)} %get-tuple-element.517, f32[2,544,512]{2,1,0:T(8,128)} %get-tuple-element.518, f32[2,544,512]{2,1,0:T(8,128)} %get-tuple-element.519, f32[2,544,512]{2,1,0:T(8,128)} %get-tuple-element.520, ...), kind=kLoop, calls=%fused_computation.120 | loop fusion | flops 14106624 | bytes 58056704 | tf_op jit(solution)/shard_map/transpose(jvp())/add_any | solution.py:51
  542.6 7.8 fusion.76
  557.0 3.6 multiply_reduce_fusion.2
  594.0 6.9 fusion.71
  611.8 221.0 %while.32 = (s32[]{:T(128)}, f32[512]{0:T(512)}, f32[512]{0:T(512)}, f32[512,8,64]{0,2,1:T(8,128)}, bf16[2,544,1536]{2,1,0:T(8,128)(2,1)}, /*index=5*/f32[2,544,...) while((s32[]{:T(128)}, f32[512]{0:T(512)}, ...), condition=%wide.region_63.64_spmd.clone, body=%wide.region_59.63_spmd.clone.sunk | while | flops 7341285888 | bytes 249676272 | solution.py:363
  626.4 5.7 subtract_exponential_fusion.2
  634.3 6.8 fusion.264
  641.1 18.9 %fusion.267 = (f32[8,64]{1,0:T(8,128)}, f32[544,8,64]{0,2,1:T(8,128)}) fusion(bf16[544,8,64]{0,2,1:T(8,128)(2,1)} %bitcast.276, f32[8,544,544]{1,2,0:T(8,128)} %subtract_exponential_fusion.2, f32[8,544,544]{1,2,0:T(8,128)} %fusion.264), kind=kOutput, calls=%fused_computation.370.clone.1 | convolution fusion | flops 322261280 | bytes 20613120 | tf_op jit(solution)/shard_map/while/body/eval_jaxpr/hij,jhd->ihd/dot_general | solution.py:153
  660.0 20.7 %fusion.265 = f32[8,544,512]{2,1,0:T(8,128)} fusion(f32[8,544,544]{1,2,0:T(8,128)} %subtract_exponential_fusion.2, f32[8,544,544]{1,2,0:T(8,128)} %fusion.264, bf16[544,256]{1,0:T(8,128)(2,1)} %copy-done.34, bf16[544,256]{1,0:T(8,128)(2,1)S(1)} %get-tuple-element.744), kind=kOutput, calls=%fused_computation.46.clone.1 | convolution fusion | flops 2444366592 | bytes 28409856 | tf_op jit(solution)/shard_map/while/body/eval_jaxpr/hij,je->hie/dot_general | solution.py:157
  680.6 4.4 subtract_convert_fusion.4
  689.2 17.5 %fusion.270 = bf16[8,64,544]{2,1,0:T(8,128)(2,1)} fusion(bf16[544,8,64]{0,2,1:T(8,128)(2,1)S(1)} %bitcast.272, f32[8,544,544]{1,2,0:T(8,128)} %subtract_exponential_fusion.2, f32[8,544,544]{1,2,0:T(8,128)} %fusion.264), kind=kOutput, calls=%fused_computation.44.clone.1 | convolution fusion | flops 321983264 | bytes 20054016 | tf_op jit(solution)/shard_map/while/body/eval_jaxpr/hij,ihd->jhd/dot_general | solution.py:156
  706.7 6.2 fusion.269
  737.0 5.6 subtract_exponential_fusion.2
  744.8 6.8 fusion.264
  751.6 18.5 %fusion.267 = (f32[8,64]{1,0:T(8,128)}, f32[544,8,64]{0,2,1:T(8,128)}) fusion(bf16[544,8,64]{0,2,1:T(8,128)(2,1)} %bitcast.276, f32[8,544,544]{1,2,0:T(8,128)} %subtract_exponential_fusion.2, f32[8,544,544]{1,2,0:T(8,128)} %fusion.264), kind=kOutput, calls=%fused_computation.370.clone.1 | convolution fusion | flops 322261280 | bytes 20613120 | tf_op jit(solution)/shard_map/while/body/eval_jaxpr/hij,jhd->ihd/dot_general | solution.py:153
  770.0 20.7 %fusion.265 = f32[8,544,512]{2,1,0:T(8,128)} fusion(f32[8,544,544]{1,2,0:T(8,128)} %subtract_exponential_fusion.2, f32[8,544,544]{1,2,0:T(8,128)} %fusion.264, bf16[544,256]{1,0:T(8,128)(2,1)} %copy-done.34, bf16[544,256]{1,0:T(8,128)(2,1)S(1)} %get-tuple-element.744), kind=kOutput, calls=%fused_computation.46.clone.1 | convolution fusion | flops 2444366592 | bytes 28409856 | tf_op jit(solution)/shard_map/while/body/eval_jaxpr/hij,je->hie/dot_general | solution.py:157
  790.7 4.3 subtract_convert_fusion.4
  799.2 17.5 %fusion.270 = bf16[8,64,544]{2,1,0:T(8,128)(2,1)} fusion(bf16[544,8,64]{0,2,1:T(8,128)(2,1)S(1)} %bitcast.272, f32[8,544,544]{1,2,0:T(8,128)} %subtract_exponential_fusion.2, f32[8,544,544]{1,2,0:T(8,128)} %fusion.264), kind=kOutput, calls=%fused_computation.44.clone.1 | convolution fusion | flops 321983264 | bytes 20054016 | tf_op jit(solution)/shard_map/while/body/eval_jaxpr/hij,ihd->jhd/dot_general | solution.py:156
  816.7 6.1 fusion.269
  832.9 5.7 multiply_reduce_fusion.3
  842.6 6.7 fusion.66
  849.5 4.4 multiply_reduce_fusion.4
  854.3 5.9 convolution_convert_fusion.1
  866.8 7.1 fusion.70
  876.6 3.9 fusion.69
  887.1 146.7 %reduce-scatter.3.cloned.1.call-done = bf16[32,6784]{1,0:T(8,128)(2,1)} async-done(((bf16[512,6784]{1,0:T(8,128)(2,1)}), bf16[32,6784]{1,0:T(8,128)(2,1)}) %reduce-scatter.3.cloned.1.call-update) | async-done | bytes 434192 | tf_op jit(solution)/shard_map/reduce_scatter | solution.py:403
  1037.5 20.2 %all-reduce.72.cloned.1.call-done = (bf16[32,6784]{1,0:T(8,128)(2,1)}, bf16[32,5760]{1,0:T(8,128)(2,1)}) async-done(((bf16[32,6784]{1,0:T(8,128)(2,1)}, bf16[32,5760]{1,0:T(8,128)(2,1)}), (bf16[32,6784]{1,0:T(8,128)(2,1)}, bf16[32,5760]{1,0:T(8,128)(2,1)})) %all-reduce.72.cloned.1.call-update) | async-done | bytes 802832 | tf_op jit(solution)/shard_map/psum | solution.py:405
  (636 shorter events, 247.2 us)
Async XLA Ops:
  7.2 6.7 copy-start.19
  7.2 95.7 %all-gather.5.cloned.1.call-start = ((), (), s32[]{:S(2)}) async-start(), calls=%async_computation.3 | async-start | bytes 6127616 | tf_op jit(solution)/shard_map/all_gather | solution.py:254
  10.1 194.6 %all-gather.3.cloned.1.call-start = ((), (), s32[]{:S(2)}) async-start(), calls=%async_computation.2 | async-start | bytes 7380992 | tf_op jit(solution)/shard_map/all_gather | solution.py:253
  13.8 873.3 %reduce-scatter.5.cloned.1.call-start = ((), (), s32[]{:S(2)}) async-start(), calls=%async_computation.5 | async-start | bytes 6266880 | tf_op jit(solution)/shard_map/reduce_scatter | solution.py:341
  14.2 204.8 %copy-start.95 = (f32[1088]{0:T(1024)}, f32[1088]{0:T(1024)S(1)}, u32[]{:S(2)}) copy-start(f32[1088]{0:T(1024)S(1)} %div.131) | copy-start | bytes 13060
  14.9 94.6 %copy-start.107 = (f32[1088]{0:T(1024)}, f32[1088]{0:T(1024)S(1)}, u32[]{:S(2)}) copy-start(f32[1088]{0:T(1024)S(1)} %add.478) | copy-start | bytes 13060
  14.9 204.1 %copy-start.93 = (f32[1088]{0:T(1024)}, f32[1088]{0:T(1024)S(1)}, u32[]{:S(2)}) copy-start(f32[1088]{0:T(1024)S(1)} %rsqrt.58) | copy-start | bytes 13060
  207.1 11.9 %copy-start.114 = (f32[512]{0:T(512)}, f32[512]{0:T(512)S(1)}, u32[]{:S(2)}) copy-start(f32[512]{0:T(512)S(1)} %get-tuple-element.385) | copy-start | bytes 6148
  207.1 34.8 %copy-start.109 = (f32[512]{0:T(512)}, f32[512]{0:T(512)S(1)}, u32[]{:S(2)}) copy-start(f32[512]{0:T(512)S(1)} %get-tuple-element.384) | copy-start | bytes 6148
  219.0 19.7 %copy-start.41 = (bf16[16,4,32,512]{3,2,1,0:T(8,128)(2,1)}, bf16[16,4,32,512]{3,2,1,0:T(8,128)(2,1)S(1)}, u32[]{:S(2)}) copy-start(bf16[16,4,32,512]{3,2,1,0:T(8,128)(2,1)S(1)} %copy.258) | copy-start | bytes 6291460
  219.5 19.2 %copy-start.47 = (bf16[1088,512]{1,0:T(8,128)(2,1)}, bf16[1088,512]{1,0:T(8,128)(2,1)S(1)}, u32[]{:S(2)}) copy-start(bf16[1088,512]{1,0:T(8,128)(2,1)S(1)} %multiply_convert_fusion.10) | copy-start | bytes 3342340
  241.4 7.6 copy-start.5
  241.4 7.6 copy-start.83
  241.9 7.1 copy-start.97
  241.9 7.1 copy-start.85
  249.0 8.0 slice-start.4
  249.0 9.1 copy-start.90
  307.9 10.1 copy-start.7
  318.1 79.5 %copy-start.150 = (f32[512]{0:T(512)S(1)}, f32[512]{0:T(512)}, u32[]{:S(2)}) copy-start(f32[512]{0:T(512)} %get-tuple-element.382) | copy-start | bytes 6148
  402.0 8.3 copy-start.25
  402.7 7.7 copy-start.43
  419.9 7.7 copy-start.26
  427.6 6.8 copy-start.157
  496.6 7.7 copy-start.8
  496.6 18.5 %slice-start.5 = ((s8[4456448]{0:T(1024)(128)(4,1)}), s8[4194304]{0:T(1024)(128)(4,1)S(1)}, s32[]{:S(2)}) async-start(s8[4456448]{0:T(1024)(128)(4,1)} %bitcast.369), calls=%async_computation.12 | async-start | bytes 8388608
  504.3 10.8 %slice-start.6 = ((s8[4456448]{0:T(1024)(128)(4,1)}), s8[262144]{0:T(1024)(128)(4,1)S(1)}, s32[]{:S(2)}) async-start(s8[4456448]{0:T(1024)(128)(4,1)} %bitcast.369), calls=%async_computation.13 | async-start | bytes 524288
  573.4 14.6 %copy-start.44 = (bf16[2048,512]{1,0:T(8,128)(2,1)S(1)}, bf16[2048,512]{1,0:T(8,128)(2,1)}, u32[]{:S(2)}) copy-start(bf16[2048,512]{1,0:T(8,128)(2,1)} %convolution_convert_fusion.4) | copy-start | bytes 6291460
  594.0 6.9 copy-start.24
  594.0 6.9 copy-start.30
  594.0 6.9 copy-start.111
  601.3 7.7 copy-start.11
  608.9 424.9 %reduce-scatter.3.cloned.1.call-start = ((), (), s32[]{:S(2)}) async-start(), calls=%async_computation.4 | async-start | bytes 7380992 | tf_op jit(solution)/shard_map/reduce_scatter | solution.py:403
  706.7 6.2 copy-start.2
  706.7 6.2 copy-start.21
  816.7 6.1 copy-start.2
  816.7 6.1 copy-start.21
  832.8 5.7 copy-start.6
  832.8 5.7 copy-start.84
  832.8 5.7 copy-start.86
  840.2 9.2 slice-start.2
  840.5 8.9 copy-start.31
  842.6 6.8 copy-start.20
  842.6 6.8 slice-start.3
  842.6 6.8 copy-start.94
  842.6 6.8 copy-start.96
  842.6 6.8 copy-start.115
  866.8 7.1 copy-start.33
  883.9 173.8 %all-reduce.72.cloned.1.call-start = ((), (), s32[]{:S(2)}) async-start(), calls=%async_computation.6 | async-start | bytes 1605632 | tf_op jit(solution)/shard_map/psum | solution.py:405
  (144 other events, 433.3 us)
Sparse Core Ops, SparseCore 0:
  10.8 92.1 all-gather.4
  106.2 98.4 all-gather.2
  609.0 144.3 reduce-scatter.4
  884.0 149.6 reduce-scatter.2
  1036.1 21.5 all-reduce.71
